TPU v7x, 512 devices: a whole 4x8x8 slice. The times are simulated.
512 devices in a mesh: seq: 32 (over x, z_hi, core), fsdp: 16 (over z_lo, y).
Axes of the slice: x: 4, y: 8, z: 8 (z_hi: 4, z_lo: 2; z = z_hi * 2 + z_lo), core: 2. Of those that a mesh axis runs over, the one named last changes fastest.
Arguments:
- hidden: bfloat16 [16, 4096, 5120], P('fsdp', 'seq'), may hold values from -6 to 6
- step_index: int32 [16], P('fsdp'), may hold values from 0 to 3
- block_sizes: int32 [16, 6], P('fsdp'), may hold values from 1 to 3, 16 in all within a row
- teacher_mod: float32 [4, 2, 5120], P(None, None, 'fsdp'), may hold values from -3 to 3
- critic_mod: float32 [4, 2, 5120], P(None, None, 'fsdp'), may hold values from -3 to 3
- teacher_weights: bfloat16 [3, 5120, 128], P(None, 'fsdp'), may hold values from -0.16699219 to 0.16699219
- critic_weights: bfloat16 [3, 5120, 128], P(None, 'fsdp'), may hold values from -0.16699219 to 0.16699219
Outputs:
- score_gap: float32 [16, 4096, 128], P('fsdp', 'seq')
Inputs may be any that keep to these rules, and one draw needn't show every extreme that they name: `block_sizes`: each clip's frame counts sum to 16, and some block of every clip holds exactly 3 frames.
All inputs are finite; a program needn't handle non-finite values.
Results may differ from a plain program's by a relative error of at most 0.012.
The roundings to bfloat16 on the way count: a program that leaves them out, or rounds other values in their place, can miss the bound.
Values may be sent and summed in bfloat16 or wider, within the bound.
A program may use at most 64 MiB of HBM per device.

v0:
```python
import jax
import jax.numpy as jnp
from jax import lax
from jax.sharding import PartitionSpec as P

FRAMES = 16


def modulate(normed, table, step):
    pick = (jnp.arange(table.shape[0], dtype=jnp.int32) == step)[:, None]
    shift = jnp.sum(jnp.where(pick, table[:, 0, :], jnp.float32(0.0)), axis=0)
    scale = jnp.sum(jnp.where(pick, table[:, 1, :], jnp.float32(0.0)), axis=0)
    return (normed * (1.0 + scale) + shift).astype(jnp.bfloat16)


def add_rows(x_mod, piece):
    return jnp.einsum("td,jdh->tjh", x_mod, piece, preferred_element_type=jnp.float32)


def attend(query, keys, values, query_blocks, key_blocks, head_size):
    scores = jnp.dot(query, keys.T, preferred_element_type=jnp.float32) / jnp.sqrt(
        jnp.float32(head_size)
    )
    visible = key_blocks[None, :] <= query_blocks[:, None]
    scores = jnp.where(visible, scores, -jnp.inf)
    top = jnp.max(scores, axis=1, keepdims=True)
    expo = jnp.where(visible, jnp.exp(scores - top), jnp.float32(0.0))
    denom = jnp.sum(expo, axis=1, keepdims=True)
    return jnp.dot(expo.astype(jnp.bfloat16), values, preferred_element_type=jnp.float32) / denom


def per_device(
    hidden, step_index, block_sizes, teacher_mod, critic_mod, teacher_weights, critic_weights
):
    rows = hidden[0]
    tok_rows = rows.shape[0]
    head_size = teacher_weights.shape[2]
    wide = rows.astype(jnp.float32)
    mean = jnp.mean(wide, axis=1, keepdims=True)
    var = jnp.mean((wide - mean) ** 2, axis=1, keepdims=True)
    normed = (wide - mean) / jnp.sqrt(var + 1e-06)
    table_t, table_c = (
        lax.all_gather(teacher_mod, "fsdp", axis=2, tiled=True),
        lax.all_gather(critic_mod, "fsdp", axis=2, tiled=True),
    )
    x_teacher = modulate(normed, table_t, step_index[0])
    x_critic = modulate(normed, table_c, step_index[0])
    proj_t = add_rows(x_teacher, lax.all_gather(teacher_weights, "fsdp", axis=1, tiled=True))
    proj_c = add_rows(x_critic, lax.all_gather(critic_weights, "fsdp", axis=1, tiled=True))
    proj_t = proj_t.astype(jnp.bfloat16)
    proj_c = proj_c.astype(jnp.bfloat16)
    clip_len = tok_rows * lax.axis_size("seq")
    frame_tok = clip_len // FRAMES
    ends = jnp.cumsum(block_sizes[0]) * frame_tok
    key_places = jnp.arange(clip_len, dtype=jnp.int32)
    key_blocks = jnp.sum((ends[None, :] <= key_places[:, None]).astype(jnp.int32), axis=1)
    query_places = lax.axis_index("seq") * tok_rows + jnp.arange(tok_rows, dtype=jnp.int32)
    query_blocks = jnp.sum((ends[None, :] <= query_places[:, None]).astype(jnp.int32), axis=1)
    keys_t, values_t = (
        lax.all_gather(proj_t[:, 1], "seq", axis=0, tiled=True),
        lax.all_gather(proj_t[:, 2], "seq", axis=0, tiled=True),
    )
    out_t = attend(proj_t[:, 0], keys_t, values_t, query_blocks, key_blocks, head_size)
    keys_c, values_c = (
        lax.all_gather(proj_c[:, 1], "seq", axis=0, tiled=True),
        lax.all_gather(proj_c[:, 2], "seq", axis=0, tiled=True),
    )
    out_c = attend(proj_c[:, 0], keys_c, values_c, query_blocks, key_blocks, head_size)
    return (out_c - out_t)[None]


def solution(mesh):
    return jax.shard_map(
        per_device,
        mesh=mesh,
        in_specs=(
            P("fsdp", "seq", None),
            P("fsdp"),
            P("fsdp", None),
            P(None, None, "fsdp"),
            P(None, None, "fsdp"),
            P(None, "fsdp", None),
            P(None, "fsdp", None),
        ),
        out_specs=P("fsdp", "seq", None),
        check_vma=False,
    )
```

profile of v0, /device:TPU:1, one launch (start us, length us, event | category | flops | bytes accessed | tf_op | source)
XLA Modules:
  0.0 489.7 jit_solution(5480213679893117160)
XLA Ops:
  6.5 0.7 all-gather.13.cloned.1.call-update
  7.3 0.7 all-gather.11.cloned.1.call-update
  8.1 0.9 copy.18
  9.0 105.1 %all_gather.24 = f32[4,2,5120]{0,1,2:T(2,128)S(1)} all-gather(f32[4,2,320]{0,1,2:T(2,128)S(1)} %copy.18), channel_id=1, replica_groups=mesh['seq'=32,'fsdp'=16] {'fsdp'}, dimensions={2}, use_global_device_ids=true | all-gather | bytes 174080 | tf_op jit(solution)/shard_map/all_gather | solution.py:44
  114.1 4.9 %fusion.52 = (f32[4,1,5120]{0,1,2:T(1,128)S(1)}, f32[4,1,5120]{0,1,2:T(1,128)}) fusion(f32[4,2,5120]{0,1,2:T(2,128)S(1)} %all_gather.24), kind=kLoop, calls=%fused_computation.70 | loop fusion | bytes 327680 | tf_op jit(solution)/shard_map/slice | solution.py:12
  119.0 4.7 copy.20
  123.7 1.4 copy.24
  125.3 98.2 %all_gather.28 = f32[4,2,5120]{0,1,2:T(2,128)S(1)} all-gather(f32[4,2,320]{0,1,2:T(2,128)S(1)} %copy.21), channel_id=1, replica_groups=mesh['seq'=32,'fsdp'=16] {'fsdp'}, dimensions={2}, use_global_device_ids=true | all-gather | bytes 174080 | tf_op jit(solution)/shard_map/all_gather | solution.py:43
  223.5 4.9 %fusion.53 = (f32[4,1,5120]{0,1,2:T(1,128)S(1)}, f32[4,1,5120]{0,1,2:T(1,128)}) fusion(f32[4,2,5120]{0,1,2:T(2,128)S(1)} %all_gather.28), kind=kLoop, calls=%fused_computation.71 | loop fusion | bytes 327680 | tf_op jit(solution)/shard_map/slice | solution.py:11
  228.5 4.7 copy.25
  233.2 1.4 copy.26
  235.7 1.6 convert_reduce_fusion
  237.8 3.0 fusion.24
  241.6 3.0 fusion.27
  246.8 58.7 %all-gather.19.cloned.1.call-done = bf16[4096,1,128]{2,0,1:T(8,128)(2,1)} async-done(((bf16[128,1,128]{2,0,1:T(8,128)(2,1)}), bf16[4096,1,128]{2,0,1:T(8,128)(2,1)}) %all-gather.19.cloned.1.call-update) | async-done | bytes 1048592 | tf_op jit(solution)/shard_map/all_gather | solution.py:60
  305.5 1.7 fusion.57
  307.2 56.6 %all-gather.15.cloned.1.call-done = bf16[4096,1,128]{2,0,1:T(8,128)(2,1)} async-done(((bf16[128,1,128]{2,0,1:T(8,128)(2,1)}), bf16[4096,1,128]{2,0,1:T(8,128)(2,1)}) %all-gather.15.cloned.1.call-update) | async-done | bytes 1048592 | tf_op jit(solution)/shard_map/all_gather | solution.py:65
  363.8 1.7 fusion.56
  365.6 1.4 copy-done
  366.9 1.0 fusion.8
  367.9 54.2 %all-gather.17.cloned.1.call-done = bf16[4096,1,128]{2,0,1:T(8,128)(2,1)} async-done(((bf16[128,1,128]{2,0,1:T(8,128)(2,1)}), bf16[4096,1,128]{2,0,1:T(8,128)(2,1)}) %all-gather.17.cloned.1.call-update) | async-done | bytes 1048592 | tf_op jit(solution)/shard_map/all_gather | solution.py:66
  422.1 2.4 convolution_divide_fusion.1
  424.5 55.9 %all-gather.21.cloned.1.call-done = bf16[4096,1,128]{2,0,1:T(8,128)(2,1)} async-done(((bf16[128,1,128]{2,0,1:T(8,128)(2,1)}), bf16[4096,1,128]{2,0,1:T(8,128)(2,1)}) %all-gather.21.cloned.1.call-update) | async-done | bytes 1048592 | tf_op jit(solution)/shard_map/all_gather | solution.py:61
  480.4 2.4 fusion.31
  (34 shorter events, 4.0 us)
Async XLA Ops:
  6.5 231.3 %all-gather.13.cloned.1.call-start = ((), (), s32[]{:S(2)}) async-start(), calls=%async_computation.1 | async-start | bytes 4177920 | tf_op jit(solution)/shard_map/all_gather | solution.py:48
  7.3 234.3 %all-gather.11.cloned.1.call-start = ((), (), s32[]{:S(2)}) async-start(), calls=%async_computation | async-start | bytes 4177920 | tf_op jit(solution)/shard_map/all_gather | solution.py:49
  8.0 297.5 %all-gather.19.cloned.1.call-start = ((), (), s32[]{:S(2)}) async-start(), calls=%async_computation.4 | async-start | bytes 1081344 | tf_op jit(solution)/shard_map/all_gather | solution.py:60
  119.0 6.1 %copy-start.2 = (f32[4,2,320]{2,1,0:T(2,128)S(1)}, f32[4,2,320]{2,1,0:T(2,128)}, u32[]{:S(2)}) copy-start(f32[4,2,320]{2,1,0:T(2,128)} %param.10) | copy-start | bytes 30724
  234.6 2.7 copy-start.1
  241.5 122.3 %all-gather.15.cloned.1.call-start = ((), (), s32[]{:S(2)}) async-start(), calls=%async_computation.2 | async-start | bytes 1081344 | tf_op jit(solution)/shard_map/all_gather | solution.py:65
  241.6 4.9 copy-start.3
  245.3 176.8 %all-gather.17.cloned.1.call-start = ((), (), s32[]{:S(2)}) async-start(), calls=%async_computation.3 | async-start | bytes 1081344 | tf_op jit(solution)/shard_map/all_gather | solution.py:66
  245.9 234.6 %all-gather.21.cloned.1.call-start = ((), (), s32[]{:S(2)}) async-start(), calls=%async_computation.5 | async-start | bytes 1081344 | tf_op jit(solution)/shard_map/all_gather | solution.py:61
  365.6 1.4 copy-start
Sparse Core Ops, SparseCore 0:
  9.4 97.2 all-gather.12
  108.9 92.1 all-gather.10
  241.6 63.8 all-gather.18
  308.5 55.2 all-gather.14
  366.8 55.2 all-gather.16
  425.1 55.2 all-gather.20
where the time goes:
time: 490 us
  waiting for transfers between devices  228 us (47%)
  blocking collectives  203 us (41%)
  local copies, waits for them, and re-layouts  25.8 us (5%)
  matrix products  14.4 us (3%)
  between operations  14.4 us (3%)
    all_gather x1, blocking collectives, per_device(): lax.all_gather(critic_mod, 'fsdp', axis=2, tiled=True)  105 us
    all_gather x1, blocking collectives, per_device(): lax.all_gather(teacher_mod, 'fsdp', axis=2, tiled=True)  98.2 us
    all_gather x1, waiting for transfers between devices, per_device(): lax.all_gather(proj_t[:, 1], 'seq', axis=0, tiled=True)  58.7 us
    all_gather x1, waiting for transfers between devices, per_device(): lax.all_gather(proj_c[:, 1], 'seq', axis=0, tiled=True)  56.6 us
    all_gather x1, waiting for transfers between devices, per_device(): lax.all_gather(proj_t[:, 2], 'seq', axis=0, tiled=True)  55.9 us
    all_gather x1, waiting for transfers between devices, per_device(): lax.all_gather(proj_c[:, 2], 'seq', axis=0, tiled=True)  54.2 us
    unnamed x13, local copies, waits for them, and re-layouts  9.98 us
  transfers between devices with their start and end apart: 6, of which 4 were waited for; matrix products, arithmetic and copies ran while one was open for 8% of the time, Pallas kernels for 0%

commit v1 on v0

v1 whole, which is shorter than its diff:
```python
import jax
import jax.numpy as jnp
from jax import lax
from jax.experimental import pallas as pl
from jax.experimental.pallas import tpu as pltpu
from jax.sharding import PartitionSpec as P

MESH = pl.DeviceIdType.MESH
NX, NY, NZ = 4, 8, 8
D, HD, TOK = 5120, 128, 128
SH = D // 16
QR = SH // NX
STEPS, BLKS = 4, 6
FT = 2 * TOK
HIDE = -1e30
QUERY, KEY, VALUE = 0, 1, 2
F32, BF16 = jnp.float32, jnp.bfloat16
RING = {0: (0,), 1: (-1, 1), 2: (-2, 2), 3: (-3, 3), 4: (4,)}
Z_UP = (0, -1, 2, -3)


def device(x, y, z, core):
    x, y, z = lax.rem(x + NX, NX), lax.rem(y + NY, NY), lax.rem(z + NZ, NZ)
    return ((x * 4 + lax.div(z, 2)) * 2 + core, lax.rem(z, 2) * NY + y)


def kernel(
    hid, step_ref, sizes_ref, tmod, cmod, tw, cw, out,
    H, N, X, W, T, ACC, KB, VT, QB, OA, ML, OS, OR, MR, FX,
    loc, hsem, ys, yr, zs, zr, xs, xr, as_, ar, bs, br, os_, or_, fsem,
):
    seq, fsdp = lax.axis_index("seq"), lax.axis_index("fsdp")
    core, zh, x = lax.rem(seq, 2), lax.rem(lax.div(seq, 2), 4), lax.div(seq, 8)
    y, zl = lax.rem(fsdp, NY), lax.div(fsdp, NY)
    z = zh * 2 + zl
    up, down = device(x, y + 1, z, core), device(x, y - 1, z, core)
    zup, zdown = device(x, y, z + 1, core), device(x, y, z - 1, core)
    zup2, zdown2 = device(x, y, z + 2, core), device(x, y, z - 2, core)
    xup, xdown, xfar = (device(x + k, y, z, core) for k in (1, -1, 2))
    other = device(x, y, z, 1 - core)
    peers = (up, down, zup, zdown, zup2, zdown2, xup, xdown, xfar, other)

    def shard(par, delta):
        side = zl if par == 0 else 1 - zl
        return side * NY + lax.rem(y + delta + NY, NY)

    own = shard(0, 0)
    started = []

    def send(src, dst, ssem, rsem, to):
        copy = pltpu.make_async_remote_copy(
            src_ref=src, dst_ref=dst, send_sem=ssem, recv_sem=rsem, device_id=to, device_id_type=MESH
        )
        copy.start()
        started.append(copy)

    def arrived(ref, rsem):
        pltpu.make_async_remote_copy(
            src_ref=ref, dst_ref=ref, send_sem=rsem, recv_sem=rsem, device_id=other, device_id_type=MESH
        ).wait_recv()

    take_h = pltpu.make_async_copy(hid.at[0], H.at[0], loc.at[0])
    take_h.start()

    @pl.when(core == 0)
    def _():
        pltpu.make_async_copy(tw, W.at[own], loc.at[1]).start()
        pltpu.make_async_copy(tmod, T.at[own], loc.at[2]).start()

    @pl.when(core == 1)
    def _():
        pltpu.make_async_copy(cw, W.at[own], loc.at[1]).start()
        pltpu.make_async_copy(cmod, T.at[own], loc.at[2]).start()

    barrier = pltpu.get_barrier_semaphore()
    for peer in peers:
        pl.semaphore_signal(barrier, inc=1, device_id=peer, device_id_type=MESH)
    pltpu.make_async_copy(tw, W.at[own], loc.at[1]).wait()
    pltpu.make_async_copy(tmod, T.at[own], loc.at[2]).wait()
    pl.semaphore_wait(barrier, len(peers))

    def quarter(d, k):
        return W.at[d, QUERY, pl.ds(pl.multiple_of(lax.rem(x + k + NX, NX) * QR, 16), QR)]

    def piece(what, d):
        if what == "q":
            return quarter(d, 0)
        if what == "t":
            return T.at[d]
        return W.at[d, KEY if what == "k" else VALUE]

    kinds = ("q", "t", "k", "v")
    ysems, zsems, xsems = {}, {}, {}

    def ysem(what, delta):
        return ysems.setdefault((what, delta), len(ysems))

    def zsem(what, delta):
        return zsems.setdefault((what, delta), len(zsems))

    def xsem(par, delta, k):
        return xsems.setdefault((par, delta, k), len(xsems))

    def ysend(what, delta, to):
        there = delta - to
        if there == -4:
            there = 4
        i = ysem(what, there)
        ref = piece(what, shard(0, delta))
        send(ref, ref, ys.at[i], yr.at[i], up if to == 1 else down)

    def zsend(what, delta):
        if what == "q":
            to = zup if delta in Z_UP else zdown
        else:
            to = zdown if what == "v" else zup
        i = zsem(what, delta)
        ref = piece(what, shard(0, delta))
        send(ref, ref, zs.at[i], zr.at[i], to)

    def xsend(par, delta, far=0):
        d = shard(par, delta)
        for k in (1, -1) if far == 0 else (far,):
            there = -k if far == 0 else 2
            i = xsem(par, delta, there)
            ref = quarter(d, 0 if far == 0 else -far)
            send(ref, ref, xs.at[i], xr.at[i], xup if k == 1 else xdown)

    def y_step(s):
        for what in kinds:
            for delta in RING[s]:
                if s > 0:
                    arrived(piece(what, shard(0, delta)), yr.at[ysem(what, delta)])
                d_ = delta
                if s == 0:
                    ysend(what, 0, 1)
                    ysend(what, 0, -1)
                elif s < 3:
                    ysend(what, d_, 1 if d_ < 0 else -1)
                elif s == 3 and (d_ > 0) == (what == "v"):
                    ysend(what, d_, 1 if d_ < 0 else -1)
                zsend(what, d_)
                if what == "q" and s > 0:
                    xsend(0, d_)

    def zq(s):
        for delta in RING[s]:
            arrived(piece("q", shard(1, delta)), zr.at[zsem("q", delta)])
            xsend(1, delta)

    def x_near(par, s):
        for delta in RING[s]:
            d = shard(par, delta)
            arrived(quarter(d, -1), xr.at[xsem(par, delta, -1)])
            if par == 0:
                xsend(par, delta, 1)
            arrived(quarter(d, 1), xr.at[xsem(par, delta, 1)])
            if par == 1:
                xsend(par, delta, -1)

    def x_far(par, s):
        for delta in RING[s]:
            arrived(quarter(shard(par, delta), 2), xr.at[xsem(par, delta, 2)])

    def norm_rows(slot):
        def body(i, carry):
            rows = pl.ds(pl.multiple_of(i * 16, 16), 16)
            wide = H[slot, rows, :].astype(F32)
            mean = jnp.sum(wide, axis=1, keepdims=True) * F32(1.0 / D)
            dev = wide - mean
            var = jnp.sum(dev * dev, axis=1, keepdims=True) * F32(1.0 / D)
            normed = dev * (F32(1.0) / jnp.sqrt(var + F32(1e-6)))
            there = pl.ds(pl.multiple_of(slot * TOK + i * 16, 16), 16)
            for d in range(16):
                N[d, there, :] = normed[:, d * SH : (d + 1) * SH]
            return carry

        lax.fori_loop(0, TOK // 16, body, 0)

    ACC[...] = jnp.zeros_like(ACC)
    step = step_ref[0]

    def project(par, s):
        def one(d):
            shift, scale = T[d, 0, 0:1, :], T[d, 0, 1:2, :]
            for k in range(1, STEPS):
                shift = jnp.where(step == k, T[d, k, 0:1, :], shift)
                scale = jnp.where(step == k, T[d, k, 1:2, :], scale)
            mod = (N[d] * (F32(1.0) + scale) + shift).astype(BF16)
            X[d] = mod
            ACC[KEY] += jnp.dot(mod, W[d, KEY], preferred_element_type=F32)
            ACC[VALUE] += jnp.dot(mod, W[d, VALUE], preferred_element_type=F32)

        if len(RING[s]) == 1:
            one(shard(par, RING[s][0]))
        else:

            def body(i, carry):
                one(shard(par, s * (2 * i - 1)))
                return carry

            lax.fori_loop(0, 2, body, 0)

    def z_step(s):
        for delta in RING[s]:
            for what in ("t", "k", "v"):
                arrived(piece(what, shard(1, delta)), zr.at[zsem(what, delta)])
        project(1, s)

    y_step(0)
    send(hid.at[0], H.at[1], hsem.at[0], hsem.at[1], other)
    take_h.wait()
    norm_rows(0)
    y_step(1)
    zq(0)
    arrived(H.at[1], hsem.at[1])
    norm_rows(1)
    y_step(2)
    zq(1)
    x_near(1, 0)
    x_near(0, 1)
    project(0, 0)
    project(0, 1)
    z_step(0)
    y_step(3)
    zq(2)
    x_near(1, 1)
    x_near(0, 2)
    project(0, 2)
    z_step(1)
    y_step(4)
    zq(3)
    x_near(1, 2)
    x_near(0, 3)
    project(0, 3)
    project(0, 4)
    zq(4)
    x_near(1, 3)
    x_near(0, 4)
    z_step(2)
    x_near(1, 4)
    z_step(3)
    z_step(4)

    KB[0] = ACC[KEY].astype(BF16)
    send(KB.at[0], KB.at[3], as_.at[0], ar.at[0], zup2)
    send(KB.at[0], KB.at[1], as_.at[1], ar.at[1], zdown2)
    VT[0] = ACC[VALUE].T.astype(BF16)
    send(VT.at[0], VT.at[3], as_.at[2], ar.at[2], zup2)
    send(VT.at[0], VT.at[1], as_.at[3], ar.at[3], zdown2)

    for s in range(5):
        if s > 0:
            x_far(0, s)
        x_far(1, s)

    def query(d, carry):
        ACC[QUERY] += jnp.dot(X[d], W[d, QUERY], preferred_element_type=F32)
        return carry

    lax.fori_loop(0, 16, query, 0)
    QB[0] = ACC[QUERY].astype(BF16)
    send(QB.at[0], QB.at[2], bs.at[1], br.at[1], xfar)
    send(QB.at[0], QB.at[3], bs.at[0], br.at[0], xup)
    send(QB.at[0], QB.at[1], bs.at[2], br.at[2], xdown)

    ends = []
    total = jnp.int32(0)
    for j in range(BLKS):
        total = total + sizes_ref[0, j]
        ends.append(total)

    def block_of(frame):
        number = jnp.int32(0)
        for end in ends:
            number = number + jnp.where(end <= frame, jnp.int32(1), jnp.int32(0))
        return number

    root = F32(1.0 / 128.0**0.5)

    def attend(r, slot, first):
        key_block = block_of(x * 4 + lax.rem(zh + slot, 4))
        query_block = block_of(lax.rem(x + r, NX) * 4 + zh)
        bias = jnp.where(key_block <= query_block, F32(0.0), F32(HIDE))
        s = lax.dot_general(KB[slot], QB[r], (((1,), (1,)), ((), ())), preferred_element_type=F32)
        s = s * root + bias
        top = jnp.max(s, axis=0, keepdims=True)
        if not first:
            before = ML[r, 0:1, :]
            top = jnp.maximum(top, before)
            keep = jnp.exp(before - top)
        e = jnp.exp(s - top)
        den = jnp.sum(e, axis=0, keepdims=True)
        o = jnp.dot(VT[slot], e.astype(BF16), preferred_element_type=F32)
        if not first:
            den = den + keep * ML[r, 1:2, :]
            o = o + keep * OA[r]
        ML[r, 0:1, :] = top
        ML[r, 1:2, :] = den
        OA[r] = o

    def attend_planes(slot, first=False):
        def body(r, carry):
            attend(r, slot, first)
            return carry

        lax.fori_loop(0, 4, body, 0)

    arrived(KB.at[3], ar.at[0])
    send(KB.at[3], KB.at[2], as_.at[4], ar.at[4], zup2)
    arrived(KB.at[1], ar.at[1])
    arrived(VT.at[3], ar.at[2])
    arrived(VT.at[1], ar.at[3])
    send(VT.at[1], VT.at[2], as_.at[5], ar.at[5], zdown2)
    for r in (1, 2, 3):
        arrived(QB.at[r], br.at[3 - r])
    attend_planes(0, first=True)
    attend_planes(1)
    attend_planes(3)
    arrived(KB.at[2], ar.at[4])
    arrived(VT.at[2], ar.at[5])

    for r, to in ((2, xfar), (1, xup), (3, xdown)):
        attend(r, 2, False)
        OS[r - 1] = OA[r].astype(BF16)
        send(OS.at[r - 1], OR.at[3 - r], os_.at[r - 1], or_.at[r - 1], to)
        send(ML.at[r], MR.at[3 - r], os_.at[r + 2], or_.at[r + 2], to)
    attend(0, 2, False)
    for r in (2, 1, 3):
        arrived(OR.at[3 - r], or_.at[r - 1])
        arrived(MR.at[3 - r], or_.at[r + 2])
    top = ML[0, 0:1, :]
    for i in range(3):
        top = jnp.maximum(top, MR[i, 0:1, :])
    w = jnp.exp(ML[0, 0:1, :] - top)
    den, o = w * ML[0, 1:2, :], w * OA[0]
    for i in range(3):
        w = jnp.exp(MR[i, 0:1, :] - top)
        den = den + w * MR[i, 1:2, :]
        o = o + w * OR[i].astype(F32)
    o = (o / den).T
    FX[0] = o[TOK:, :]
    send(FX.at[0], FX.at[1], fsem.at[0], fsem.at[1], other)
    arrived(FX.at[1], fsem.at[1])
    sign = jnp.where(core == 0, F32(1.0), F32(-1.0))
    out[0] = (FX[1] - o[:TOK, :]) * sign

    for copy in started:
        copy.wait_send()


def per_device(hidden, step_index, block_sizes, teacher_mod, critic_mod, teacher_weights, critic_weights):
    vmem, smem, hbm = (pl.BlockSpec(memory_space=m) for m in (pltpu.VMEM, pltpu.SMEM, pl.ANY))
    dma = pltpu.SemaphoreType.DMA
    return pl.pallas_call(
        kernel,
        out_shape=jax.ShapeDtypeStruct((1, TOK, HD), F32),
        in_specs=[hbm, smem, smem, hbm, hbm, hbm, hbm],
        out_specs=vmem,
        scratch_shapes=[
            pltpu.VMEM((2, TOK, D), BF16),
            pltpu.VMEM((16, FT, SH), F32),
            pltpu.VMEM((16, FT, SH), BF16),
            pltpu.VMEM((16, 3, SH, HD), BF16),
            pltpu.VMEM((16, STEPS, 2, SH), F32),
            pltpu.VMEM((3, FT, HD), F32),
            pltpu.VMEM((4, FT, HD), BF16),
            pltpu.VMEM((4, HD, FT), BF16),
            pltpu.VMEM((4, FT, HD), BF16),
            pltpu.VMEM((4, HD, FT), F32),
            pltpu.VMEM((4, 8, FT), F32),
            pltpu.VMEM((3, HD, FT), BF16),
            pltpu.VMEM((3, HD, FT), BF16),
            pltpu.VMEM((3, 8, FT), F32),
            pltpu.VMEM((2, TOK, HD), F32),
            dma((3,)),
            dma((2,)),
            dma((28,)),
            dma((28,)),
            dma((32,)),
            dma((32,)),
            dma((45,)),
            dma((45,)),
            dma((6,)),
            dma((6,)),
            dma((3,)),
            dma((3,)),
            dma((6,)),
            dma((6,)),
            dma((2,)),
        ],
        compiler_params=pltpu.CompilerParams(
            collective_id=0, has_side_effects=True, vmem_limit_bytes=48 * 2**20
        ),
        cost_estimate=pl.CostEstimate(flops=3 * 10**9, bytes_accessed=4 * 10**6, transcendentals=10**6),
    )(hidden, step_index, block_sizes, teacher_mod, critic_mod, teacher_weights, critic_weights)


def solution(mesh):
    return jax.shard_map(
        per_device,
        mesh=mesh,
        in_specs=(
            P("fsdp", "seq", None),
            P("fsdp"),
            P("fsdp", None),
            P(None, None, "fsdp"),
            P(None, None, "fsdp"),
            P(None, "fsdp", None),
            P(None, "fsdp", None),
        ),
        out_specs=P("fsdp", "seq", None),
        check_vma=False,
    )
```

time: 490 us -> 71.1 us (0.15)
  waiting for transfers between devices: 228 us -> 0 us
  blocking collectives: 203 us -> 0 us
  Pallas kernels: 0 us -> 64.2 us
  local copies, waits for them, and re-layouts: 25.8 us -> 5.9 us
  matrix products: 14.4 us -> 0 us
  between operations: 14.4 us -> 0.67 us
    all_gather x6 -> x0, waiting for transfers between devices: 225 us -> none  [the longest x1 58.7 us: per_device(): lax.all_gather(proj_t[:, 1], 'seq', axis=0, tiled=True)]
    all_gather x2 -> x0, blocking collectives: 203 us -> none  [the longest x1 105 us: per_device(): lax.all_gather(critic_mod, 'fsdp', axis=2, tiled=True)]
    pallas_call x0 -> x1, Pallas kernels: none -> 64.2 us  [per_device(): pl.pallas_call(kernel, out_shape=jax.ShapeDtypeStruct((1, TOK, HD), F32),...]
    slice x5 -> x0, local copies, waits for them, and re-layouts: 15.8 us -> none  [the longest x2 9.63 us: modulate(): shift = jnp.sum(jnp.where(pick, table[:, 0, :], jnp.float32(0.0)), axis=0)]
    dot_general x6 -> x0, matrix products: 14.4 us -> none  [the longest x2 6.05 us: add_rows(): jnp.einsum('td,jdh->tjh', x_mod, piece, preferred_element_type=jnp.float32)]
  transfers between devices with their start and end apart: 6 -> 0, of which waited for: 4 -> 0; matrix products, arithmetic and copies ran while one was open for 8% -> 0% of each run, Pallas kernels for 0% -> 0%
where the time goes in v1:
time: 71.1 us; the launch traced here: 70.8 us
  Pallas kernels  64.2 us (90%)
  local copies, waits for them, and re-layouts  5.9 us (8%)
    pallas_call x1, Pallas kernels, per_device(): pl.pallas_call(kernel, out_shape=jax.ShapeDtypeStruct((1, TOK, HD), F32),...  64.2 us
    unnamed x13, local copies, waits for them, and re-layouts  5.9 us

profile of v1, /device:TPU:1, one launch (start us, length us, event | category | flops | bytes accessed | tf_op | source)
XLA Modules:
  0.0 70.8 jit_solution(784990142306231169)
XLA Ops:
  0.7 0.0 copy-start
  0.7 1.3 %copy-done = bf16[1,128,5120]{2,1,0:T(8,128)(2,1)S(1)} copy-done((bf16[1,128,5120]{2,1,0:T(8,128)(2,1)S(1)}, bf16[1,128,5120]{2,1,0:T(8,128)(2,1)}, u32[]{:S(2)}) %copy-start) | copy-done | bytes 1310744
  2.0 0.0 copy-start.1
  2.0 0.9 %copy-done.1 = bf16[3,320,128]{2,1,0:T(8,128)(2,1)S(1)} copy-done((bf16[3,320,128]{2,1,0:T(8,128)(2,1)S(1)}, bf16[3,320,128]{2,1,0:T(8,128)(2,1)}, u32[]{:S(2)}) %copy-start.1) | copy-done | bytes 245784
  2.9 0.0 copy-start.2
  2.9 0.9 %copy-done.2 = bf16[3,320,128]{2,1,0:T(8,128)(2,1)S(1)} copy-done((bf16[3,320,128]{2,1,0:T(8,128)(2,1)S(1)}, bf16[3,320,128]{2,1,0:T(8,128)(2,1)}, u32[]{:S(2)}) %copy-start.2) | copy-done | bytes 245784
  3.9 0.0 copy-start.3
  3.9 0.7 copy-done.3
  4.6 0.0 copy-start.4
  4.6 0.7 copy-done.4
  5.3 0.0 copy-start.5
  5.3 0.7 copy-done.5
  5.9 64.2 %shard_map.73 = f32[1,128,128]{2,1,0:T(8,128)S(1)} custom-call(bf16[1,128,5120]{2,1,0:T(8,128)(2,1)S(1)} %copy-done, s32[1]{0:T(128)S(6)} %copy.9.step_ref, s32[1,6]{1,0:T(1,128)S(1)} %copy-done.5, f32[4,2,320]{2,1,0:T(2,128)S(1)} %copy-done.3, f32[4,2,320]{2,1,0:T(2,128)S(1)} %copy-done.4, bf16[3,320,128]{2,1,0:T(8,128)(2,1)S(1)} %copy-done.1, ...), custom_call_target="tpu_custom_call" | custom-call | flops 3000000000 | bytes 4000000 | tf_op jit(solution)/shard_map/pallas_call | solution.py:355
  70.2 0.6 copy.10
Async XLA Ops:
  0.7 1.3 %copy-start = (bf16[1,128,5120]{2,1,0:T(8,128)(2,1)S(1)}, bf16[1,128,5120]{2,1,0:T(8,128)(2,1)}, u32[]{:S(2)}) copy-start(bf16[1,128,5120]{2,1,0:T(8,128)(2,1)} %hid.1) | copy-start | bytes 3932164
  2.0 0.9 %copy-start.1 = (bf16[3,320,128]{2,1,0:T(8,128)(2,1)S(1)}, bf16[3,320,128]{2,1,0:T(8,128)(2,1)}, u32[]{:S(2)}) copy-start(bf16[3,320,128]{2,1,0:T(8,128)(2,1)} %tw.1) | copy-start | bytes 737284
  2.9 0.9 %copy-start.2 = (bf16[3,320,128]{2,1,0:T(8,128)(2,1)S(1)}, bf16[3,320,128]{2,1,0:T(8,128)(2,1)}, u32[]{:S(2)}) copy-start(bf16[3,320,128]{2,1,0:T(8,128)(2,1)} %cw.1) | copy-start | bytes 737284
  3.9 0.7 copy-start.3
  4.6 0.7 copy-start.4
  5.3 0.7 copy-start.5

commit v2 on v1

v2 whole, which is shorter than its diff:
```python
import jax
import jax.numpy as jnp
from jax import lax
from jax.experimental import pallas as pl
from jax.experimental.pallas import tpu as pltpu
from jax.sharding import PartitionSpec as P

MESH = pl.DeviceIdType.MESH
NX, NY, NZ = 4, 8, 8
D, HD, TOK = 5120, 128, 128
SH = D // 16
QR = SH // NX
STEPS, BLKS = 4, 6
QMODE, S4 = 2, False
PARTS = 4
FT = 2 * TOK
HIDE = -1e30
QUERY, KEY, VALUE = 0, 1, 2
F32, BF16 = jnp.float32, jnp.bfloat16
RING = {0: (0,), 1: (-1, 1), 2: (-2, 2), 3: (-3, 3), 4: (4,)}
Z_UP = (0, -1, 2, -3)


def device(x, y, z, core):
    x, y, z = lax.rem(x + NX, NX), lax.rem(y + NY, NY), lax.rem(z + NZ, NZ)
    return ((x * 4 + lax.div(z, 2)) * 2 + core, lax.rem(z, 2) * NY + y)


def kernel(
    hid, step_in, sizes_in, tmod, cmod, tw, cw, out,
    H, MEAN, RSTD, X, W, T, AKV, AQ, KB, VT, QB, OA, ML, OS, OR, MR, FX, step_ref, sizes_ref,
    loc, hsem, ys, yr, zs, zr, xs, xr, as_, ar, bs, br, os_, or_, fsem,
):
    seq, fsdp = lax.axis_index("seq"), lax.axis_index("fsdp")
    core, zh, x = lax.rem(seq, 2), lax.rem(lax.div(seq, 2), 4), lax.div(seq, 8)
    y, zl = lax.rem(fsdp, NY), lax.div(fsdp, NY)
    z = zh * 2 + zl
    zup, zdown = device(x, y, z + 1, core), device(x, y, z - 1, core)
    zup2, zdown2 = device(x, y, z + 2, core), device(x, y, z - 2, core)
    xup, xdown, xfar = (device(x + k, y, z, core) for k in (1, -1, 2))
    other = device(x, y, z, 1 - core)
    peers = [device(x, y + k, z, core) for k in ((1, -1), (1, -1, 2, -2, 3, -3, 4), (1, -1, 2, -2))[QMODE]]
    peers += [zup, zdown, zup2, zdown2, xup, xdown, xfar, other]

    def shard(par, delta):
        side = zl if par == 0 else 1 - zl
        return side * NY + lax.rem(y + delta + NY, NY)

    own = shard(0, 0)
    started = []

    def send(src, dst, ssem, rsem, to):
        copy = pltpu.make_async_remote_copy(
            src_ref=src, dst_ref=dst, send_sem=ssem, recv_sem=rsem, device_id=to, device_id_type=MESH
        )
        copy.start()
        started.append(copy)

    def arrived(ref, rsem):
        pltpu.make_async_remote_copy(
            src_ref=ref, dst_ref=ref, send_sem=rsem, recv_sem=rsem, device_id=other, device_id_type=MESH
        ).wait_recv()

    take_h = pltpu.make_async_copy(hid.at[0], H.at[pl.ds(0, TOK)], loc.at[0])
    take_h.start()
    take_step = pltpu.make_async_copy(step_in, step_ref, loc.at[3])
    take_step.start()
    take_sizes = pltpu.make_async_copy(sizes_in, sizes_ref, loc.at[4])
    take_sizes.start()

    @pl.when(core == 0)
    def _():
        pltpu.make_async_copy(tw, W.at[own], loc.at[1]).start()
        pltpu.make_async_copy(tmod, T.at[own], loc.at[2]).start()

    @pl.when(core == 1)
    def _():
        pltpu.make_async_copy(cw, W.at[own], loc.at[1]).start()
        pltpu.make_async_copy(cmod, T.at[own], loc.at[2]).start()

    barrier = pltpu.get_barrier_semaphore()
    for peer in peers:
        pl.semaphore_signal(barrier, inc=1, device_id=peer, device_id_type=MESH)
    pltpu.make_async_copy(tw, W.at[own], loc.at[1]).wait()
    pltpu.make_async_copy(tmod, T.at[own], loc.at[2]).wait()
    take_step.wait()
    take_sizes.wait()

    def rows_of(k):
        return pl.ds(pl.multiple_of(lax.rem(x + k + NX, NX) * QR, 16), QR)

    def quarter(d, delta, k=0):
        return W.at[d, pl.ds(0, 3 if S4 and delta == 4 else 1), rows_of(k)]

    def piece(what, d, delta):
        if what == "q":
            return quarter(d, delta)
        if what == "t":
            return T.at[d]
        rows = pl.ds(int(what[1]) * (SH // PARTS), SH // PARTS)
        return W.at[d, KEY if what[0] == "k" else VALUE, rows]

    parts = [kind + str(i) for kind in "kv" for i in range(PARTS)]
    ysems, zsems, xsems = {}, {}, {}

    def ysem(what, delta):
        return ysems.setdefault((what, delta), len(ysems))

    def zsem(what, delta):
        return zsems.setdefault((what, delta), len(zsems))

    def xsem(par, delta, k):
        return xsems.setdefault((par, delta, k), len(xsems))

    def ysend(what, delta, hops):
        there = 4 if abs(delta - hops) == 4 else delta - hops
        i = ysem(what, there)
        ref = piece(what, shard(0, delta), there if what == "q" else delta)
        send(ref, ref, ys.at[i], yr.at[i], device(x, y + hops, z, core))

    def yget(what, delta):
        arrived(piece(what, shard(0, delta), delta), yr.at[ysem(what, delta)])

    def zsend(what, delta):
        if what == "q":
            to = zup if delta in Z_UP else zdown
        else:
            to = zdown if what[0] == "v" else zup
        i = zsem(what, delta)
        ref = piece(what, shard(0, delta), delta)
        send(ref, ref, zs.at[i], zr.at[i], to)

    def zget(what, delta):
        arrived(piece(what, shard(1, delta), delta), zr.at[zsem(what, delta)])

    def xsend(par, delta):
        for k, to in ((1, xup), (-1, xdown), (2, xfar)):
            i = xsem(par, delta, -k if k != 2 else 2)
            ref = quarter(shard(par, delta), delta)
            send(ref, ref, xs.at[i], xr.at[i], to)

    def x_get(par, s):
        for delta in RING[s]:
            for k in (-1, 1, 2):
                arrived(quarter(shard(par, delta), delta, k), xr.at[xsem(par, delta, k)])

    def q_step(s):
        for delta in RING[s]:
            yget("q", delta)
            way = 1 if delta < 0 else -1
            if QMODE == 0 and (s < 3 or delta == -3) or QMODE == 2 and s == 2:
                ysend("q", delta, way)
            if QMODE == 2 and delta == -2:
                ysend("q", delta, 2)
            zsend("q", delta)
            xsend(0, delta)

    def q_cross(s):
        for delta in RING[s]:
            zget("q", delta)
            xsend(1, delta)

    def halfway(what):
        return -1 if what[0] == "v" else 1

    def ring(whats, s):
        for what in whats:
            for delta in RING[s]:
                yget(what, delta)
                way = 1 if delta < 0 else -1
                if s < 3 or (s == 3 and way == halfway(what) and not S4):
                    ysend(what, delta, way)
                zsend(what, delta)

    def cross(whats, s):
        for delta in RING[s]:
            for what in whats:
                zget(what, delta)

    def start_sends():
        for way in (1, -1):
            ysend("t", 0, way)
        for hops in ((1, -1), (4, 1, -1, 2, -2, 3, -3), (2, -2, 1, -1))[QMODE]:
            ysend("q", 0, hops)
        if S4:
            ysend("t", 0, 4)
        zsend("t", 0)
        zsend("q", 0)
        for what in parts:
            for way in (1, -1):
                ysend(what, 0, way)
            zsend(what, 0)

    def norm_rows(first, last):
        def body(i, carry):
            rows = pl.ds(pl.multiple_of(i * 16, 16), 16)
            wide = H[rows, :].astype(F32)
            mean = jnp.sum(wide, axis=1, keepdims=True) * F32(1.0 / D)
            dev = wide - mean
            var = jnp.sum(dev * dev, axis=1, keepdims=True) * F32(1.0 / D)
            MEAN[rows, :] = jnp.broadcast_to(mean, (16, 128))
            RSTD[rows, :] = jnp.broadcast_to(F32(1.0) / jnp.sqrt(var + F32(1e-6)), (16, 128))
            return carry

        lax.fori_loop(first, last, body, 0)

    step = step_ref[0]

    def pair(par, i):
        side = zl if par == 0 else 1 - zl
        turn = 1 - 2 * lax.rem(y, 2)
        k = (0, -turn, turn, 2)[i]
        return side * 4 + lax.rem(lax.div(y, 2) + k + 4, 4)

    def modulate(par, i):
        p = pair(par, i)

        def rows_at(j):
            halves = []
            for h in range(2):
                row = T[2 * p + h, 0, j : j + 1, :]
                for k in range(1, STEPS):
                    row = jnp.where(step == k, T[2 * p + h, k, j : j + 1, :], row)
                halves.append(row)
            return jnp.concatenate(halves, axis=1)

        shift, scale = rows_at(0), F32(1.0) + rows_at(1)
        for r in range(0, FT, 64):
            rows = pl.ds(r, 64)
            wide = H[rows, pl.ds(pl.multiple_of(p * 2 * SH, 128), 2 * SH)].astype(F32)
            mean = jnp.concatenate([MEAN[rows, :]] * 5, axis=1)
            rstd = jnp.concatenate([RSTD[rows, :]] * 5, axis=1)
            X[p, rows, :] = ((wide - mean) * rstd * scale + shift).astype(BF16)

    def slab(p, j):
        return W[pl.ds(2 * p, 2), j].reshape(2 * SH, HD)

    def project(par, i):
        p = pair(par, i)
        w = jnp.concatenate([slab(p, KEY), slab(p, VALUE)], axis=1)
        AKV[...] += jnp.dot(X[p], w, preferred_element_type=F32)

    def query(par, i):
        p = pair(par, i)
        AQ[...] += jnp.dot(X[p], slab(p, QUERY), preferred_element_type=F32)

    def queries(par):
        if par == 1:
            x_get(par, 0)
        for i in range(4):
            x_get(par, i + 1)
            query(par, i)

    def send_kv():
        KB[0] = AKV[:, :HD].astype(BF16)
        send(KB.at[0], KB.at[3], as_.at[0], ar.at[0], zup2)
        send(KB.at[0], KB.at[1], as_.at[1], ar.at[1], zdown2)
        VT[0] = AKV[:, HD:].T.astype(BF16)
        send(VT.at[0], VT.at[3], as_.at[2], ar.at[2], zup2)
        send(VT.at[0], VT.at[1], as_.at[3], ar.at[3], zdown2)

    def send_q():
        QB[0] = AQ[...].astype(BF16)
        send(QB.at[0], QB.at[2], bs.at[1], br.at[1], xfar)
        send(QB.at[0], QB.at[3], bs.at[0], br.at[0], xup)
        send(QB.at[0], QB.at[1], bs.at[2], br.at[2], xdown)

    pl.semaphore_wait(barrier, len(peers))
    start_sends()
    send(hid.at[0], H.at[pl.ds(TOK, TOK)], hsem.at[0], hsem.at[1], other)
    take_h.wait()
    norm_rows(0, 8)
    AKV[...] = jnp.zeros_like(AKV)
    AQ[...] = jnp.zeros_like(AQ)
    ring(("t",),1)
    q_step(1)
    q_step(2)
    arrived(H.at[pl.ds(TOK, TOK)], hsem.at[1])
    norm_rows(8, 16)
    ring(parts,1)
    ring(("t",),2)
    q_cross(0)
    q_step(3)
    q_step(4)
    q_cross(1)
    q_cross(2)
    modulate(0, 0)
    ring(parts,2)
    ring(("t",),3)
    q_cross(3)
    q_cross(4)
    project(0, 0)
    modulate(0, 1)
    ring(parts,3)
    ring(("t",),4)
    cross(("t",),0)
    cross(("t",),1)
    project(0, 1)
    modulate(0, 2)
    modulate(0, 3)
    cross(parts,0)
    modulate(1, 0)
    ring(parts,4)
    project(0, 2)
    cross(parts,1)
    project(1, 0)
    project(0, 3)
    cross(("t",),2)
    cross(("t",),3)
    cross(("t",),4)
    modulate(1, 1)
    modulate(1, 2)
    modulate(1, 3)
    cross(parts,2)
    project(1, 1)
    cross(parts,3)
    project(1, 2)
    cross(parts,4)
    project(1, 3)
    send_kv()
    queries(0)
    queries(1)
    send_q()
    ends = []
    total = jnp.int32(0)
    for j in range(BLKS):
        total = total + sizes_ref[0, j]
        ends.append(total)

    def block_of(frame):
        number = jnp.int32(0)
        for end in ends:
            number = number + jnp.where(end <= frame, jnp.int32(1), jnp.int32(0))
        return number

    root = F32(1.0 / 128.0**0.5)

    def attend(r, slot, first):
        key_block = block_of(x * 4 + lax.rem(zh + slot, 4))
        query_block = block_of(lax.rem(x + r, NX) * 4 + zh)
        bias = jnp.where(key_block <= query_block, F32(0.0), F32(HIDE))
        s = lax.dot_general(KB[slot], QB[r], (((1,), (1,)), ((), ())), preferred_element_type=F32)
        s = s * root + bias
        top = jnp.max(s, axis=0, keepdims=True)
        if not first:
            before = ML[r, 0:1, :]
            top = jnp.maximum(top, before)
            keep = jnp.exp(before - top)
        e = jnp.exp(s - top)
        den = jnp.sum(e, axis=0, keepdims=True)
        o = jnp.dot(VT[slot], e.astype(BF16), preferred_element_type=F32)
        if not first:
            den = den + keep * ML[r, 1:2, :]
            o = o + keep * OA[r]
        ML[r, 0:1, :] = top
        ML[r, 1:2, :] = den
        OA[r] = o

    def attend_planes(slot, first=False):
        for r in range(4):
            attend(r, slot, first)

    arrived(KB.at[3], ar.at[0])
    send(KB.at[3], KB.at[2], as_.at[4], ar.at[4], zup2)
    arrived(KB.at[1], ar.at[1])
    arrived(VT.at[3], ar.at[2])
    arrived(VT.at[1], ar.at[3])
    send(VT.at[1], VT.at[2], as_.at[5], ar.at[5], zdown2)
    for r in (1, 2, 3):
        arrived(QB.at[r], br.at[3 - r])
    attend_planes(0, first=True)
    attend_planes(1)
    attend_planes(3)
    arrived(KB.at[2], ar.at[4])
    arrived(VT.at[2], ar.at[5])

    for r, to in ((2, xfar), (1, xup), (3, xdown)):
        attend(r, 2, False)
        OS[r - 1] = OA[r].astype(BF16)
        send(OS.at[r - 1], OR.at[3 - r], os_.at[r - 1], or_.at[r - 1], to)
        send(ML.at[r], MR.at[3 - r], os_.at[r + 2], or_.at[r + 2], to)
    attend(0, 2, False)
    for r in (2, 1, 3):
        arrived(OR.at[3 - r], or_.at[r - 1])
        arrived(MR.at[3 - r], or_.at[r + 2])
    top = ML[0, 0:1, :]
    for i in range(3):
        top = jnp.maximum(top, MR[i, 0:1, :])
    w = jnp.exp(ML[0, 0:1, :] - top)
    den, o = w * ML[0, 1:2, :], w * OA[0]
    for i in range(3):
        w = jnp.exp(MR[i, 0:1, :] - top)
        den = den + w * MR[i, 1:2, :]
        o = o + w * OR[i].astype(F32)
    o = (o / den).T
    FX[0] = o[TOK:, :]
    send(FX.at[0], FX.at[1], fsem.at[0], fsem.at[1], other)
    arrived(FX.at[1], fsem.at[1])
    sign = jnp.where(core == 0, F32(1.0), F32(-1.0))
    out[0] = (FX[1] - o[:TOK, :]) * sign

    for copy in started:
        copy.wait_send()


def per_device(hidden, step_index, block_sizes, teacher_mod, critic_mod, teacher_weights, critic_weights):
    vmem, hbm = (pl.BlockSpec(memory_space=m) for m in (pltpu.VMEM, pltpu.HBM))
    dma = pltpu.SemaphoreType.DMA
    return pl.pallas_call(
        kernel,
        out_shape=jax.ShapeDtypeStruct((1, TOK, HD), F32),
        in_specs=[hbm] * 7,
        out_specs=vmem,
        scratch_shapes=[
            pltpu.VMEM((FT, D), BF16),
            pltpu.VMEM((FT, 128), F32),
            pltpu.VMEM((FT, 128), F32),
            pltpu.VMEM((8, FT, 2 * SH), BF16),
            pltpu.VMEM((16, 3, SH, HD), BF16),
            pltpu.VMEM((16, STEPS, 2, SH), F32),
            pltpu.VMEM((FT, 2 * HD), F32),
            pltpu.VMEM((FT, HD), F32),
            pltpu.VMEM((4, FT, HD), BF16),
            pltpu.VMEM((4, HD, FT), BF16),
            pltpu.VMEM((4, FT, HD), BF16),
            pltpu.VMEM((4, HD, FT), F32),
            pltpu.VMEM((4, 8, FT), F32),
            pltpu.VMEM((3, HD, FT), BF16),
            pltpu.VMEM((3, HD, FT), BF16),
            pltpu.VMEM((3, 8, FT), F32),
            pltpu.VMEM((2, TOK, HD), F32),
            pltpu.SMEM((1,), jnp.int32),
            pltpu.SMEM((1, BLKS), jnp.int32),
            dma((5,)),
            dma((2,)),
            dma((72,)),
            dma((72,)),
            dma((80,)),
            dma((80,)),
            dma((45,)),
            dma((45,)),
            dma((6,)),
            dma((6,)),
            dma((3,)),
            dma((3,)),
            dma((6,)),
            dma((6,)),
            dma((2,)),
        ],
        compiler_params=pltpu.CompilerParams(
            collective_id=0, has_side_effects=True, vmem_limit_bytes=63 * 2**20
        ),
        cost_estimate=pl.CostEstimate(flops=3 * 10**9, bytes_accessed=4 * 10**6, transcendentals=10**6),
    )(hidden, step_index, block_sizes, teacher_mod, critic_mod, teacher_weights, critic_weights)


def solution(mesh):
    return jax.shard_map(
        per_device,
        mesh=mesh,
        in_specs=(
            P("fsdp", "seq", None),
            P("fsdp"),
            P("fsdp", None),
            P(None, None, "fsdp"),
            P(None, None, "fsdp"),
            P(None, "fsdp", None),
            P(None, "fsdp", None),
        ),
        out_specs=P("fsdp", "seq", None),
        check_vma=False,
    )
```

time: 71.1 us -> 62.3 us (0.88)
  local copies, waits for them, and re-layouts: 5.9 us -> 1.47 us
  Pallas kernels: 64.2 us -> 59.9 us
    unnamed x13 -> x1, local copies, waits for them, and re-layouts: 5.9 us -> 1.47 us
    pallas_call x1, Pallas kernels: 64.2 us -> 59.9 us  [per_device(): pl.pallas_call(kernel, out_shape=jax.ShapeDtypeStruct((1, TOK, HD), F32),...]
where the time goes in v2:
time: 62.3 us; the launch traced here: 62.1 us
  Pallas kernels  59.9 us (96%)
  local copies, waits for them, and re-layouts  1.47 us (2%)
  between operations  0.66 us (1%)
    pallas_call x1, Pallas kernels, per_device(): pl.pallas_call(kernel, out_shape=jax.ShapeDtypeStruct((1, TOK, HD), F32),...  59.9 us
    unnamed x1, local copies, waits for them, and re-layouts  1.47 us

profile of v2, /device:TPU:1, one launch (start us, length us, event | category | flops | bytes accessed | tf_op | source)
XLA Modules:
  0.0 62.1 jit_solution(838518953876805845)
XLA Ops:
  0.7 59.9 %shard_map.73 = f32[1,128,128]{2,1,0:T(8,128)} custom-call(bf16[1,128,5120]{2,1,0:T(8,128)(2,1)} %hid.1, s32[1]{0:T(128)S(6)} %copy.9.step_in, s32[1,6]{1,0:T(1,128)} %sizes_in.1, f32[4,2,320]{2,1,0:T(2,128)} %tmod.1, f32[4,2,320]{2,1,0:T(2,128)} %cmod.1, bf16[3,320,128]{2,1,0:T(8,128)(2,1)} %tw.1, bf16[3,320,128]{2,1,0:T(8,128)(2,1)} %cw.1), custom_call_target="tpu_custom_call" | custom-call | flops 3000000000 | bytes 4000000 | tf_op jit(solution)/shard_map/pallas_call | solution.py:409
  60.6 1.5 %copy.10 = f32[1,128,128]{2,1,0:T(8,128)} copy(f32[1,128,128]{2,1,0:T(8,128)} %shard_map.73) | data formatting | bytes 131072

commit v3 on v2

--- a/solution.py
+++ b/solution.py
@@ -11,7 +11,7 @@
 SH = D // 16
 QR = SH // NX
 STEPS, BLKS = 4, 6
-QMODE, S4 = 2, False
+QMODE, S4, SPLIT = 2, False, False
 PARTS = 4
 FT = 2 * TOK
 HIDE = -1e30
@@ -28,19 +28,24 @@
 
 def kernel(
     hid, step_in, sizes_in, tmod, cmod, tw, cw, out,
-    H, MEAN, RSTD, X, W, T, AKV, AQ, KB, VT, QB, OA, ML, OS, OR, MR, FX, step_ref, sizes_ref,
-    loc, hsem, ys, yr, zs, zr, xs, xr, as_, ar, bs, br, os_, or_, fsem,
+    H, MEAN, RSTD, X, W, T, AKV, AQ, KB, VT, QB, OA, ML, OS, OR, MR, OF, step_ref, sizes_ref,
+    loc, hsem, ys, yr, zs, zr, xs, xr, as_, ar, bs, br, os_, or_, ms, mr,
 ):
     seq, fsdp = lax.axis_index("seq"), lax.axis_index("fsdp")
     core, zh, x = lax.rem(seq, 2), lax.rem(lax.div(seq, 2), 4), lax.div(seq, 8)
     y, zl = lax.rem(fsdp, NY), lax.div(fsdp, NY)
     z = zh * 2 + zl
     zup, zdown = device(x, y, z + 1, core), device(x, y, z - 1, core)
-    zup2, zdown2 = device(x, y, z + 2, core), device(x, y, z - 2, core)
+    along_x = core if SPLIT else 0 * core
+    along_z = 1 - along_x
+    kup, kdown = (device(x + k * along_x, y, z + 2 * k * along_z, core) for k in (1, -1))
+    qup, qdown, qfar = (
+        [device(x + k * along_z, y, z + 2 * k * along_x, c) for c in (core, 1 - core)] for k in (1, -1, 2)
+    )
     xup, xdown, xfar = (device(x + k, y, z, core) for k in (1, -1, 2))
     other = device(x, y, z, 1 - core)
-    peers = [device(x, y + k, z, core) for k in ((1, -1), (1, -1, 2, -2, 3, -3, 4), (1, -1, 2, -2))[QMODE]]
-    peers += [zup, zdown, zup2, zdown2, xup, xdown, xfar, other]
+    peers = [device(x, y + k, z, core) for k in ((1, -1), (1, -1, 2, -2, 3, -3, 4), (1, -1, 2, -2), (1, -1, 2, -2, 4))[QMODE]]
+    peers += [device(x, y, z + k, core) for k in (2, -2)] + [zup, zdown, xup, xdown, xfar, other, qup[1], qdown[1], qfar[1]]
 
     def shard(par, delta):
         side = zl if par == 0 else 1 - zl
@@ -148,7 +153,7 @@
         for delta in RING[s]:
             yget("q", delta)
             way = 1 if delta < 0 else -1
-            if QMODE == 0 and (s < 3 or delta == -3) or QMODE == 2 and s == 2:
+            if QMODE == 0 and (s < 3 or delta == -3) or QMODE >= 2 and s == 2:
                 ysend("q", delta, way)
             if QMODE == 2 and delta == -2:
                 ysend("q", delta, 2)
@@ -180,7 +185,7 @@
     def start_sends():
         for way in (1, -1):
             ysend("t", 0, way)
-        for hops in ((1, -1), (4, 1, -1, 2, -2, 3, -3), (2, -2, 1, -1))[QMODE]:
+        for hops in ((1, -1), (4, 1, -1, 2, -2, 3, -3), (2, -2, 1, -1), (4, 1, -1, 2, -2))[QMODE]:
             ysend("q", 0, hops)
         if S4:
             ysend("t", 0, 4)
@@ -248,22 +253,25 @@
         if par == 1:
             x_get(par, 0)
         for i in range(4):
-            x_get(par, i + 1)
+            if i < 3 or not S4:
+                x_get(par, i + 1)
             query(par, i)
 
-    def send_kv():
+    def send_k():
         KB[0] = AKV[:, :HD].astype(BF16)
-        send(KB.at[0], KB.at[3], as_.at[0], ar.at[0], zup2)
-        send(KB.at[0], KB.at[1], as_.at[1], ar.at[1], zdown2)
+        send(KB.at[0], KB.at[3], as_.at[0], ar.at[0], kup)
+        send(KB.at[0], KB.at[1], as_.at[1], ar.at[1], kdown)
+
+    def send_v():
         VT[0] = AKV[:, HD:].T.astype(BF16)
-        send(VT.at[0], VT.at[3], as_.at[2], ar.at[2], zup2)
-        send(VT.at[0], VT.at[1], as_.at[3], ar.at[3], zdown2)
+        send(VT.at[0], VT.at[3], as_.at[2], ar.at[2], kup)
+        send(VT.at[0], VT.at[1], as_.at[3], ar.at[3], kdown)
 
     def send_q():
         QB[0] = AQ[...].astype(BF16)
-        send(QB.at[0], QB.at[2], bs.at[1], br.at[1], xfar)
-        send(QB.at[0], QB.at[3], bs.at[0], br.at[0], xup)
-        send(QB.at[0], QB.at[1], bs.at[2], br.at[2], xdown)
+        send(QB.at[0], QB.at[2], bs.at[1], br.at[1], qfar[0])
+        send(QB.at[0], QB.at[3], bs.at[0], br.at[0], qup[0])
+        send(QB.at[0], QB.at[1], bs.at[2], br.at[2], qdown[0])
 
     pl.semaphore_wait(barrier, len(peers))
     start_sends()
@@ -317,7 +325,8 @@
     project(1, 2)
     cross(parts,4)
     project(1, 3)
-    send_kv()
+    send_k()
+    send_v()
     queries(0)
     queries(1)
     send_q()
@@ -336,8 +345,8 @@
     root = F32(1.0 / 128.0**0.5)
 
     def attend(r, slot, first):
-        key_block = block_of(x * 4 + lax.rem(zh + slot, 4))
-        query_block = block_of(lax.rem(x + r, NX) * 4 + zh)
+        key_block = block_of(lax.rem(x + along_x * slot, 4) * 4 + lax.rem(zh + along_z * slot, 4))
+        query_block = block_of(lax.rem(x + along_z * r, 4) * 4 + lax.rem(zh + along_x * r, 4))
         bias = jnp.where(key_block <= query_block, F32(0.0), F32(HIDE))
         s = lax.dot_general(KB[slot], QB[r], (((1,), (1,)), ((), ())), preferred_element_type=F32)
         s = s * root + bias
@@ -361,11 +370,11 @@
             attend(r, slot, first)
 
     arrived(KB.at[3], ar.at[0])
-    send(KB.at[3], KB.at[2], as_.at[4], ar.at[4], zup2)
+    send(KB.at[3], KB.at[2], as_.at[4], ar.at[4], kup)
     arrived(KB.at[1], ar.at[1])
     arrived(VT.at[3], ar.at[2])
     arrived(VT.at[1], ar.at[3])
-    send(VT.at[1], VT.at[2], as_.at[5], ar.at[5], zdown2)
+    send(VT.at[1], VT.at[2], as_.at[5], ar.at[5], kdown)
     for r in (1, 2, 3):
         arrived(QB.at[r], br.at[3 - r])
     attend_planes(0, first=True)
@@ -374,30 +383,45 @@
     arrived(KB.at[2], ar.at[4])
     arrived(VT.at[2], ar.at[5])
 
-    for r, to in ((2, xfar), (1, xup), (3, xdown)):
+    def give(r, h, o_ref, to):
+        i, j = h * 4 + (4 - r) % 4, h * 4 + r
+        send(o_ref, OR.at[h, (4 - r) % 4] if r else OF, os_.at[j], or_.at[i], to)
+        send(ML.at[r, :, pl.ds(h * TOK, TOK)], MR.at[h, (4 - r) % 4], ms.at[j], mr.at[i], to)
+
+    def got(r, h):
+        arrived(OR.at[h, r] if r else OF, or_.at[h * 4 + r])
+        arrived(MR.at[h, r], mr.at[h * 4 + r])
+
+    for r, to in ((2, qfar), (1, qup), (3, qdown)):
         attend(r, 2, False)
-        OS[r - 1] = OA[r].astype(BF16)
-        send(OS.at[r - 1], OR.at[3 - r], os_.at[r - 1], or_.at[r - 1], to)
-        send(ML.at[r], MR.at[3 - r], os_.at[r + 2], or_.at[r + 2], to)
+        for h in range(2):
+            OS[r, h] = OA[r, :, h * TOK : (h + 1) * TOK].astype(BF16)
+            give(r, h, OS.at[r, h], to[h])
     attend(0, 2, False)
-    for r in (2, 1, 3):
-        arrived(OR.at[3 - r], or_.at[r - 1])
-        arrived(MR.at[3 - r], or_.at[r + 2])
-    top = ML[0, 0:1, :]
-    for i in range(3):
-        top = jnp.maximum(top, MR[i, 0:1, :])
-    w = jnp.exp(ML[0, 0:1, :] - top)
-    den, o = w * ML[0, 1:2, :], w * OA[0]
-    for i in range(3):
-        w = jnp.exp(MR[i, 0:1, :] - top)
-        den = den + w * MR[i, 1:2, :]
-        o = o + w * OR[i].astype(F32)
-    o = (o / den).T
-    FX[0] = o[TOK:, :]
-    send(FX.at[0], FX.at[1], fsem.at[0], fsem.at[1], other)
-    arrived(FX.at[1], fsem.at[1])
+    give(0, 1, OA.at[0, :, pl.ds(TOK, TOK)], other)
+
+    def combine(h):
+        own = ML[0, :, :TOK] if h == 0 else MR[1, 0]
+        parts_ = [own] + [MR[h, r] for r in (1, 2, 3)]
+        top = parts_[0][0:1, :]
+        for part in parts_[1:]:
+            top = jnp.maximum(top, part[0:1, :])
+        den, o = F32(0.0), F32(0.0)
+        for r, part in enumerate(parts_):
+            w = jnp.exp(part[0:1, :] - top)
+            den = den + w * part[1:2, :]
+            if r == 0:
+                o = o + w * (OA[0, :, :TOK] if h == 0 else OF[...])
+            else:
+                o = o + w * OR[h, r].astype(F32)
+        return o / den
+
+    got(0, 1)
+    for r in (1, 3, 2):
+        for h in range(2):
+            got(r, h)
     sign = jnp.where(core == 0, F32(1.0), F32(-1.0))
-    out[0] = (FX[1] - o[:TOK, :]) * sign
+    out[0] = ((combine(1) - combine(0)) * sign).T
 
     for copy in started:
         copy.wait_send()
@@ -425,10 +449,10 @@
             pltpu.VMEM((4, FT, HD), BF16),
             pltpu.VMEM((4, HD, FT), F32),
             pltpu.VMEM((4, 8, FT), F32),
-            pltpu.VMEM((3, HD, FT), BF16),
-            pltpu.VMEM((3, HD, FT), BF16),
-            pltpu.VMEM((3, 8, FT), F32),
-            pltpu.VMEM((2, TOK, HD), F32),
+            pltpu.VMEM((4, 2, HD, TOK), BF16),
+            pltpu.VMEM((2, 4, HD, TOK), BF16),
+            pltpu.VMEM((2, 4, 8, TOK), F32),
+            pltpu.VMEM((HD, TOK), F32),
             pltpu.SMEM((1,), jnp.int32),
             pltpu.SMEM((1, BLKS), jnp.int32),
             dma((5,)),
@@ -443,9 +467,10 @@
             dma((6,)),
             dma((3,)),
             dma((3,)),
-            dma((6,)),
-            dma((6,)),
-            dma((2,)),
+            dma((8,)),
+            dma((8,)),
+            dma((8,)),
+            dma((8,)),
         ],
         compiler_params=pltpu.CompilerParams(
             collective_id=0, has_side_effects=True, vmem_limit_bytes=63 * 2**20

time: 62.3 us -> 60.8 us (0.976)
  Pallas kernels: 59.9 us -> 58.5 us
    pallas_call x1, Pallas kernels: 59.9 us -> 58.5 us  [per_device(): pl.pallas_call(kernel, out_shape=jax.ShapeDtypeStruct((1, TOK, HD), F32),...]
where the time goes in v3:
time: 60.8 us; the launch traced here: 60.6 us
  Pallas kernels  58.5 us (96%)
  local copies, waits for them, and re-layouts  1.47 us (2%)
  between operations  0.66 us (1%)
    pallas_call x1, Pallas kernels, per_device(): pl.pallas_call(kernel, out_shape=jax.ShapeDtypeStruct((1, TOK, HD), F32),...  58.5 us
    unnamed x1, local copies, waits for them, and re-layouts  1.47 us

profile of v3, /device:TPU:1, one launch (start us, length us, event | category | flops | bytes accessed | tf_op | source)
XLA Modules:
  0.0 60.6 jit_solution(15350276995001623352)
XLA Ops:
  0.7 58.5 %shard_map.73 = f32[1,128,128]{2,1,0:T(8,128)} custom-call(bf16[1,128,5120]{2,1,0:T(8,128)(2,1)} %hid.1, s32[1]{0:T(128)S(6)} %copy.9.step_in, s32[1,6]{1,0:T(1,128)} %sizes_in.1, f32[4,2,320]{2,1,0:T(2,128)} %tmod.1, f32[4,2,320]{2,1,0:T(2,128)} %cmod.1, bf16[3,320,128]{2,1,0:T(8,128)(2,1)} %tw.1, bf16[3,320,128]{2,1,0:T(8,128)(2,1)} %cw.1), custom_call_target="tpu_custom_call" | custom-call | flops 3000000000 | bytes 4000000 | tf_op jit(solution)/shard_map/pallas_call | solution.py:433
  59.1 1.5 %copy.10 = f32[1,128,128]{2,1,0:T(8,128)} copy(f32[1,128,128]{2,1,0:T(8,128)} %shard_map.73) | data formatting | bytes 131072
